TPU v7x, 32 devices: a whole 2x2x4 slice. The times are simulated.
32 devices in a mesh: slab: 2 (over y), genome: 4 (over x, core), group: 4 (over z).
Axes of the slice: x: 2, y: 2, z: 4, core: 2. Of those that a mesh axis runs over, the one named last changes fastest.
Arguments:
- genotypes: bfloat16 [640, 12288], P(None, ('slab', 'genome', 'group')), parts along dimension 1, may hold values from -6 to 6
Outputs:
- ld_score: float32 [12288], P(('slab', 'genome', 'group')), parts along dimension 0
There are 2 independent parts, one for each index of `slab`. A program takes and returns all parts, laid end to end along the dimension named above; each array names one. Nothing has to cross between parts.
All inputs are finite; a program needn't handle non-finite values.
Results may differ from a plain program's by a relative error of at most 0.0003.
Values may be sent and summed in bfloat16 or wider, within the bound.
A program may use at most 64 MiB of HBM per device.

v0:
```python
import jax
import jax.numpy as jnp
from jax import lax
from jax.sharding import PartitionSpec as P


def passed_along(block, axis, distance):
    devices = range(lax.axis_size(axis))
    route = [(i - distance, i) for i in devices if i - distance in devices]
    return lax.ppermute(block, axis, route)


def per_device(genotypes):
    scaling = 1.0 / genotypes.shape[0]

    def squares(columns):
        band = (
            lax.dot_general(
                genotypes, columns, (((0,), (0,)), ((), ())), preferred_element_type=jnp.float32
            )
            * scaling
        )
        return jnp.sum(band * band, axis=1)

    gathered = lax.all_gather(genotypes, "group", axis=1, tiled=True)
    following = passed_along(gathered, "genome", -1)
    ld_score = squares(gathered) + squares(following)
    return ld_score


def solution(mesh):
    placed = (P(None, ("slab", "genome", "group")),)
    return jax.shard_map(
        per_device,
        mesh=mesh,
        in_specs=placed,
        out_specs=P(("slab", "genome", "group")),
        check_vma=False,
    )
```

profile of v0, /device:TPU:1, one launch (start us, length us, event | category | flops | bytes accessed | tf_op | source)
XLA Modules:
  0.0 89.7 jit_solution(2843091351955072725)
XLA Ops:
  6.5 0.0 all-gather.2.cloned.1.call-start
  6.5 0.0 copy-start
  6.5 0.7 all-gather.2.cloned.1.call-update
  7.3 47.5 %all-gather.2.cloned.1.call-done = bf16[640,1536]{1,0:T(8,128)(2,1)} async-done(((bf16[640,384]{1,0:T(8,128)(2,1)}), bf16[640,1536]{1,0:T(8,128)(2,1)}) %all-gather.2.cloned.1.call-update) | async-done | bytes 1966096 | tf_op jit(solution)/shard_map/all_gather | solution.py:25
  54.7 2.7 %collective-permute-start = (bf16[640,1536]{1,0:T(8,128)(2,1)}, bf16[640,1536]{1,0:T(8,128)(2,1)S(1)}, u32[]{:S(2)}, u32[]{:S(2)}) collective-permute-start(bf16[640,1536]{1,0:T(8,128)(2,1)} %all-gather.2.cloned.1.call-done), channel_id=1, source_target_pairs={{4,0},{8,4},{12,8},{5,1},{9,5},{13,9},{6,2},{10,6},{14,10},{7,3},{... | collective-permute-start | bytes 5898248 | tf_op jit(solution)/shard_map/ppermute | solution.py:10
  57.5 2.9 %fusion.2 = f32[384]{0:T(512)S(1)} fusion(bf16[640,384]{1,0:T(8,128)(2,1)} %param.1, bf16[640,1536]{1,0:T(8,128)(2,1)} %all-gather.2.cloned.1.call-done), kind=kOutput, calls=%fused_computation.4 | convolution fusion | flops 756743808 | bytes 2459136 | tf_op jit(solution)/shard_map/dot_general | solution.py:18
  60.4 20.7 %collective-permute-done = bf16[640,1536]{1,0:T(8,128)(2,1)S(1)} collective-permute-done((bf16[640,1536]{1,0:T(8,128)(2,1)}, bf16[640,1536]{1,0:T(8,128)(2,1)S(1)}, u32[]{:S(2)}, u32[]{:S(2)}) %collective-permute-start) | collective-permute-done | bytes 1966112 | tf_op jit(solution)/shard_map/ppermute | solution.py:10
  81.1 0.0 copy-done
  81.1 1.2 %fusion.3 = f32[384]{0:T(512)S(1)} fusion(bf16[640,384]{1,0:T(8,128)(2,1)S(1)} %copy-done, bf16[640,1536]{1,0:T(8,128)(2,1)S(1)} %collective-permute-done), kind=kOutput, calls=%fused_computation.5 | convolution fusion | flops 756743808 | bytes 2459136 | tf_op jit(solution)/shard_map/dot_general | solution.py:18
  82.2 0.6 add.3
Async XLA Ops:
  6.5 48.2 %all-gather.2.cloned.1.call-start = ((), (), s32[]{:S(2)}) async-start(), calls=%async_computation | async-start | bytes 2457600 | tf_op jit(solution)/shard_map/all_gather | solution.py:25
  6.5 74.5 %copy-start = (bf16[640,384]{1,0:T(8,128)(2,1)S(1)}, bf16[640,384]{1,0:T(8,128)(2,1)}, u32[]{:S(2)}) copy-start(bf16[640,384]{1,0:T(8,128)(2,1)} %param.1) | copy-start | bytes 1474564
  54.7 26.3 %collective-permute-start = (bf16[640,1536]{1,0:T(8,128)(2,1)}, bf16[640,1536]{1,0:T(8,128)(2,1)S(1)}, u32[]{:S(2)}, u32[]{:S(2)}) collective-permute-start(bf16[640,1536]{1,0:T(8,128)(2,1)} %all-gather.2.cloned.1.call-done), channel_id=1, source_target_pairs={{4,0},{8,4},{12,8},{5,1},{9,5},{13,9},{6,2},{10,6},{14,10},{7,3},{... | collective-permute-start | bytes 5898248 | tf_op jit(solution)/shard_map/ppermute | solution.py:10
Sparse Core Ops, SparseCore 0:
  9.0 45.7 all-gather.1
where the time goes:
time: 89.8 us; the launch traced here: 89.7 us
  waiting for transfers between devices  68.8 us (77%)
  between operations  13.4 us (15%)
  matrix products  4.09 us (5%)
  starting transfers between devices  2.75 us (3%)
    all_gather x1, waiting for transfers between devices, per_device(): gathered = lax.all_gather(genotypes, 'group', axis=1, tiled=True)  47.5 us
    ppermute x1, waiting for transfers between devices, passed_along(): return lax.ppermute(block, axis, route)  20.7 us
    dot_general x2, matrix products, squares(): lax.dot_general(genotypes, columns, (((0,), (0,)), ((), ())), preferred_e...  4.09 us
    ppermute x1, starting transfers between devices, passed_along(): return lax.ppermute(block, axis, route)  2.75 us
  transfers between devices with their start and end apart: 2, of which 2 were waited for; matrix products, arithmetic and copies ran while one was open for 3% of the time, Pallas kernels for 0%

commit v1 on v0

v1 whole, which is shorter than its diff:
```python
import functools

import jax
import jax.numpy as jnp
from jax import lax
from jax.experimental import pallas as pl
from jax.experimental.pallas import tpu as pltpu
from jax.sharding import PartitionSpec as P

MESH = pl.DeviceIdType.MESH
B = 128
SKEW = 2


def plan(samples):
    blocks = [(i, j) for i in range(samples // B) for j in range(i + 1)]
    per = 3 if len(blocks) % 3 == 0 else 1
    chunks = [list(range(k, k + per)) for k in range(0, len(blocks), per)]
    return blocks, per, chunks


def pieces(blocks, chunk):
    runs = []
    for b in chunk:
        i, j = blocks[b]
        if runs and runs[-1][0] == i:
            runs[-1][3] += 1
        else:
            runs.append([i, j, b, 1])
    return runs


def kernel(
    n, ng, mine, out, following, own, from_left, from_right, to_right, to_left,
    x_send, x_recv, r_send, r_recv, l_send, l_recv,
):
    z = lax.axis_index("group")
    g = lax.axis_index("genome")
    samples, width = mine.shape
    blocks, per, chunks = plan(samples)
    rows = samples // B

    has_left, has_right = z > 0, z < n - 1
    has_before, has_next = g > 0, g < ng - 1

    barrier = pltpu.get_barrier_semaphore()

    def greet(there, where):
        @pl.when(there)
        def _():
            pl.semaphore_signal(barrier, inc=1, device_id=where, device_id_type=MESH)

    greet(has_left, {"group": z - 1})
    greet(has_right, {"group": z + 1})
    greet(has_next, {"genome": g + 1})
    peers = jnp.minimum(z, 1) + jnp.minimum(n - 1 - z, 1) + jnp.minimum(g, 1)
    pl.semaphore_wait(barrier, peers)

    def row_copy(i):
        return pltpu.make_async_remote_copy(
            src_ref=mine.at[pl.ds(i * B, B)],
            dst_ref=following.at[pl.ds(i * B, B)],
            send_sem=x_send.at[i],
            recv_sem=x_recv.at[i],
            device_id={"genome": g - 1},
            device_id_type=MESH,
        )

    def right_copy(c):
        return pltpu.make_async_remote_copy(
            src_ref=to_right.at[pl.ds(c * per, per)],
            dst_ref=from_left.at[pl.ds(c * per, per)],
            send_sem=r_send.at[c],
            recv_sem=r_recv.at[c],
            device_id={"group": z + 1},
            device_id_type=MESH,
        )

    def left_copy(c):
        return pltpu.make_async_remote_copy(
            src_ref=to_left.at[pl.ds(c * per, per)],
            dst_ref=from_right.at[pl.ds(c * per, per)],
            send_sem=l_send.at[c],
            recv_sem=l_recv.at[c],
            device_id={"group": z - 1},
            device_id_type=MESH,
        )

    @pl.when(has_before)
    def _():
        for i in range(rows):
            row_copy(i).start()

    def products(ref, run, add):
        i, j, b, count = run
        band = lax.dot_general(
            ref[pl.ds(i * B, B), :],
            ref[pl.ds(j * B, count * B), :],
            (((1,), (1,)), ((), ())),
            preferred_element_type=jnp.float32,
        )
        for k in range(count):
            block = band[:, k * B : (k + 1) * B]
            own[b + k] = own[b + k] + block if add else block

    arrived = 0
    for t in range(len(chunks) + SKEW * (n - 1)):
        if t < len(chunks):
            runs = pieces(blocks, chunks[t])
            for run in runs:
                products(mine, run, False)
            need = runs[-1][0] + 1

            @pl.when(has_next)
            def _():
                for i in range(arrived, need):
                    row_copy(i).wait_recv()
                for run in runs:
                    products(following, run, True)

            arrived = need

        c = t - SKEW * z

        @pl.when(has_right & (c >= 0) & (c < len(chunks)))
        def _():
            span = pl.ds(c * per, per)

            @pl.when(has_left)
            def _():
                right_copy(c).wait_recv()
                total = own[span] + from_left[span].astype(jnp.float32)
                to_right[span] = total.astype(to_right.dtype)

            @pl.when(z == 0)
            def _():
                to_right[span] = own[span].astype(to_right.dtype)

            right_copy(c).start()

        d = t - SKEW * (n - 1 - z)

        @pl.when(has_left & (d >= 0) & (d < len(chunks)))
        def _():
            span = pl.ds(d * per, per)

            @pl.when(has_right)
            def _():
                left_copy(d).wait_recv()
                total = own[span] + from_right[span].astype(jnp.float32)
                to_left[span] = total.astype(to_left.dtype)

            @pl.when(z == n - 1)
            def _():
                to_left[span] = own[span].astype(to_left.dtype)

            left_copy(d).start()

    score = jnp.zeros((1, width), jnp.float32)
    for c, chunk in enumerate(chunks):
        span = pl.ds(c * per, per)

        @pl.when(has_left)
        def _():
            @pl.when(z == n - 1)
            def _():
                right_copy(c).wait_recv()

            own[span] = own[span] + from_left[span].astype(jnp.float32)

        @pl.when(has_right)
        def _():
            @pl.when(z == 0)
            def _():
                left_copy(c).wait_recv()

            own[span] = own[span] + from_right[span].astype(jnp.float32)

        for i, j, b, count in pieces(blocks, chunk):
            parts = []
            for k in range(count):
                part = own[b + k]
                parts.append(part if j + k == i else part + part)
            whole = jnp.concatenate(parts, axis=1) if count > 1 else parts[0]
            high = whole.astype(jnp.bfloat16)
            low = (whole - high.astype(jnp.float32)).astype(jnp.bfloat16)
            both = lax.dot_general(
                jnp.concatenate([high, low], axis=0),
                mine[pl.ds(j * B, count * B), :],
                (((1,), (0,)), ((), ())),
                preferred_element_type=jnp.float32,
            )
            weighed = both[:B] + both[B:]
            score = score + jnp.sum(
                weighed * mine[pl.ds(i * B, B), :].astype(jnp.float32),
                axis=0,
                keepdims=True,
            )
    out[...] = score * (1.0 / samples) * (1.0 / samples)

    @pl.when(has_before)
    def _():
        for i in range(rows):
            row_copy(i).wait_send()

    @pl.when(has_right)
    def _():
        for c in range(len(chunks)):
            right_copy(c).wait_send()

    @pl.when(has_left)
    def _():
        for c in range(len(chunks)):
            left_copy(c).wait_send()


def solution(mesh):
    n, ng = mesh.shape["group"], mesh.shape["genome"]

    def per_device(genotypes):
        samples, width = genotypes.shape
        blocks, per, chunks = plan(samples)
        steps, rows = len(chunks), samples // B
        sent = pltpu.VMEM((len(blocks), B, B), jnp.bfloat16)
        scores = pl.pallas_call(
            functools.partial(kernel, n, ng),
            out_shape=jax.ShapeDtypeStruct((1, width), jnp.float32),
            in_specs=[pl.BlockSpec(memory_space=pltpu.VMEM)],
            out_specs=pl.BlockSpec(memory_space=pltpu.VMEM),
            scratch_shapes=[
                pltpu.VMEM((samples, width), jnp.bfloat16),
                pltpu.VMEM((len(blocks), B, B), jnp.float32),
                sent,
                sent,
                sent,
                sent,
                pltpu.SemaphoreType.DMA((rows,)),
                pltpu.SemaphoreType.DMA((rows,)),
                pltpu.SemaphoreType.DMA((steps,)),
                pltpu.SemaphoreType.DMA((steps,)),
                pltpu.SemaphoreType.DMA((steps,)),
                pltpu.SemaphoreType.DMA((steps,)),
            ],
            compiler_params=pltpu.CompilerParams(
                collective_id=0,
                has_side_effects=True,
                vmem_limit_bytes=32 * 1024 * 1024,
            ),
        )(genotypes)
        return scores.reshape(width)

    return jax.shard_map(
        per_device,
        mesh=mesh,
        in_specs=(P(None, ("slab", "genome", "group")),),
        out_specs=P(("slab", "genome", "group")),
        check_vma=False,
    )
```

time: 89.8 us -> 27.9 us (0.31)
  waiting for transfers between devices: 68.8 us -> 0 us
  Pallas kernels: 0 us -> 26.1 us
  between operations: 13.4 us -> 0.01 us
  matrix products: 4.09 us -> 0 us
  starting transfers between devices: 2.75 us -> 0 us
  local copies, waits for them, and re-layouts: 0.01 us -> 1.03 us
    all_gather x1 -> x0, waiting for transfers between devices: 47.5 us -> none  [per_device(): gathered = lax.all_gather(genotypes, 'group', axis=1, tiled=True)]
    pallas_call x0 -> x1, Pallas kernels: none -> 26.1 us  [per_device(): pl.pallas_call(functools.partial(kernel, n, ng), out_shape=jax.ShapeDtype...]
    ppermute x1 -> x0, waiting for transfers between devices: 20.7 us -> none  [passed_along(): return lax.ppermute(block, axis, route)]
    dot_general x2 -> x0, matrix products: 4.09 us -> none  [squares(): lax.dot_general(genotypes, columns, (((0,), (0,)), ((), ())), preferred_e...]
    ppermute x1 -> x0, starting transfers between devices: 2.75 us -> none  [passed_along(): return lax.ppermute(block, axis, route)]
    unnamed x2, local copies, waits for them, and re-layouts: 0.01 us -> 1.03 us
  transfers between devices with their start and end apart: 2 -> 0, of which waited for: 2 -> 0; matrix products, arithmetic and copies ran while one was open for 3% -> 0% of each run, Pallas kernels for 0% -> 0%
where the time goes in v1:
time: 27.9 us; the launch traced here: 27.7 us
  Pallas kernels  26.1 us (94%)
  local copies, waits for them, and re-layouts  1.03 us (4%)
  other arithmetic  0.6 us (2%)
    pallas_call x1, Pallas kernels, per_device(): pl.pallas_call(functools.partial(kernel, n, ng), out_shape=jax.ShapeDtype...  26.1 us
    unnamed x2, local copies, waits for them, and re-layouts  1.03 us
    pallas_call x1, other arithmetic, per_device(): pl.pallas_call(functools.partial(kernel, n, ng), out_shape=jax.ShapeDtype...  0.6 us

profile of v1, /device:TPU:1, one launch (start us, length us, event | category | flops | bytes accessed | tf_op | source)
XLA Modules:
  0.0 27.7 jit_solution(3468670312634427421)
XLA Ops:
  0.0 0.0 copy-start
  0.0 1.0 %copy-done = bf16[640,384]{1,0:T(8,128)(2,1)S(1)} copy-done((bf16[640,384]{1,0:T(8,128)(2,1)S(1)}, bf16[640,384]{1,0:T(8,128)(2,1)}, u32[]{:S(2)}) %copy-start) | copy-done | bytes 491544
  1.0 26.1 %shard_map.17 = f32[1,384]{1,0:T(1,128)S(1)} custom-call(bf16[640,384]{1,0:T(8,128)(2,1)S(1)} %copy-done), custom_call_target="tpu_custom_call" | custom-call | tf_op jit(solution)/shard_map/pallas_call | solution.py:225
  27.1 0.6 %reduce = f32[384]{0:T(512)} reduce(f32[1,384]{1,0:T(1,128)S(1)} %shard_map.17, f32[]{:T(128)} %constant), dimensions={0}, to_apply=%pallas_call.3.reduce_sub_computation | reduce | bytes 3076 | tf_op jit(solution)/shard_map/pallas_call | solution.py:225
Async XLA Ops:
  0.0 1.0 %copy-start = (bf16[640,384]{1,0:T(8,128)(2,1)S(1)}, bf16[640,384]{1,0:T(8,128)(2,1)}, u32[]{:S(2)}) copy-start(bf16[640,384]{1,0:T(8,128)(2,1)} %mine.1) | copy-start | bytes 1474564

commit v2 on v1

v2 whole, which is shorter than its diff:
```python
import functools

import jax
import jax.numpy as jnp
from jax import lax
from jax.experimental import pallas as pl
from jax.experimental.pallas import tpu as pltpu
from jax.sharding import PartitionSpec as P

MESH = pl.DeviceIdType.MESH
B = 128
SKEW = 3


def triangle(rows):
    return [(i, j) for i in range(rows) for j in range(i + 1)]


def kernel(
    n, ng, given, out, mine, following, own, from_left, from_right, to_right, to_left,
    m_sem, x_send, x_recv, r_send, r_recv, l_send, l_recv,
):
    z = lax.axis_index("group")
    g = lax.axis_index("genome")
    samples, width = given.shape
    rows = samples // B
    blocks = triangle(rows)
    first = [i * (i + 1) // 2 for i in range(rows)]

    has_left, has_right = z > 0, z < n - 1
    has_before, has_next = g > 0, g < ng - 1

    barrier = pltpu.get_barrier_semaphore()

    def greet(there, where):
        @pl.when(there)
        def _():
            pl.semaphore_signal(barrier, inc=1, device_id=where, device_id_type=MESH)

    greet(has_left, {"group": z - 1})
    greet(has_right, {"group": z + 1})
    greet(has_next, {"genome": g + 1})
    def load(i):
        span = pl.ds(i * B, B)
        return pltpu.make_async_copy(given.at[span], mine.at[span], m_sem.at[i])

    for i in range(rows):
        load(i).start()

    peers = jnp.minimum(z, 1) + jnp.minimum(n - 1 - z, 1) + jnp.minimum(g, 1)
    pl.semaphore_wait(barrier, peers)

    def row_copy(i):
        return pltpu.make_async_remote_copy(
            src_ref=given.at[pl.ds(i * B, B)],
            dst_ref=following.at[pl.ds(i * B, B)],
            send_sem=x_send.at[i],
            recv_sem=x_recv.at[i],
            device_id={"genome": g - 1},
            device_id_type=MESH,
        )

    def right_copy(c):
        return pltpu.make_async_remote_copy(
            src_ref=to_right.at[c],
            dst_ref=from_left.at[c],
            send_sem=r_send.at[c],
            recv_sem=r_recv.at[c],
            device_id={"group": z + 1},
            device_id_type=MESH,
        )

    def left_copy(c):
        return pltpu.make_async_remote_copy(
            src_ref=to_left.at[c],
            dst_ref=from_right.at[c],
            send_sem=l_send.at[c],
            recv_sem=l_recv.at[c],
            device_id={"group": z - 1},
            device_id_type=MESH,
        )

    @pl.when(has_before)
    def _():
        for i in range(rows):
            row_copy(i).start()

    def products(ref, i, add):
        band = lax.dot_general(
            ref[pl.ds(i * B, B), :],
            ref[pl.ds(0, (i + 1) * B), :],
            (((1,), (1,)), ((), ())),
            preferred_element_type=jnp.float32,
        )
        for j in range(i + 1):
            block = band[:, j * B : (j + 1) * B]
            own[first[i] + j] = own[first[i] + j] + block if add else block

    for i in range(rows):
        load(i).wait()
        products(mine, i, False)

    for t in range(len(blocks) + SKEW * (n - 1)):
        if t in first:
            i = first.index(t)

            @pl.when(has_next)
            def _():
                row_copy(i).wait_recv()
                products(following, i, True)

        c = t - SKEW * z

        @pl.when(has_right & (c >= 0) & (c < len(blocks)))
        def _():
            @pl.when(has_left)
            def _():
                right_copy(c).wait_recv()
                total = own[c] + from_left[c].astype(jnp.float32)
                to_right[c] = total.astype(to_right.dtype)

            @pl.when(z == 0)
            def _():
                to_right[c] = own[c].astype(to_right.dtype)

            right_copy(c).start()

        d = t - SKEW * (n - 1 - z)

        @pl.when(has_left & (d >= 0) & (d < len(blocks)))
        def _():
            @pl.when(has_right)
            def _():
                left_copy(d).wait_recv()
                total = own[d] + from_right[d].astype(jnp.float32)
                to_left[d] = total.astype(to_left.dtype)

            @pl.when(z == n - 1)
            def _():
                to_left[d] = own[d].astype(to_left.dtype)

            left_copy(d).start()

    score = jnp.zeros((1, width), jnp.float32)
    for i in range(rows):
        span = pl.ds(first[i], i + 1)

        @pl.when(has_left)
        def _():
            @pl.when(z == n - 1)
            def _():
                for j in range(i + 1):
                    right_copy(first[i] + j).wait_recv()

            own[span] = own[span] + from_left[span].astype(jnp.float32)

        @pl.when(has_right)
        def _():
            @pl.when(z == 0)
            def _():
                for j in range(i + 1):
                    left_copy(first[i] + j).wait_recv()

            own[span] = own[span] + from_right[span].astype(jnp.float32)

        parts = []
        for j in range(i + 1):
            part = own[first[i] + j]
            parts.append(part if j == i else part + part)
        whole = jnp.concatenate(parts, axis=1) if i else parts[0]
        high = whole.astype(jnp.bfloat16)
        low = (whole - high.astype(jnp.float32)).astype(jnp.bfloat16)
        both = lax.dot_general(
            jnp.concatenate([high, low], axis=0),
            mine[pl.ds(0, (i + 1) * B), :],
            (((1,), (0,)), ((), ())),
            preferred_element_type=jnp.float32,
        )
        weighed = both[:B] + both[B:]
        score = score + jnp.sum(
            weighed * mine[pl.ds(i * B, B), :].astype(jnp.float32),
            axis=0,
            keepdims=True,
        )
    out[...] = (score * (1.0 / samples) * (1.0 / samples)).reshape(width)

    @pl.when(has_before)
    def _():
        for i in range(rows):
            row_copy(i).wait_send()

    @pl.when(has_right)
    def _():
        for c in range(len(blocks)):
            right_copy(c).wait_send()

    @pl.when(has_left)
    def _():
        for c in range(len(blocks)):
            left_copy(c).wait_send()


def solution(mesh):
    n, ng = mesh.shape["group"], mesh.shape["genome"]

    def per_device(genotypes):
        samples, width = genotypes.shape
        rows = samples // B
        steps = len(triangle(rows))
        sent = pltpu.VMEM((steps, B, B), jnp.bfloat16)
        return pl.pallas_call(
            functools.partial(kernel, n, ng),
            out_shape=jax.ShapeDtypeStruct((width,), jnp.float32),
            in_specs=[pl.BlockSpec(memory_space=pl.ANY)],
            out_specs=pl.BlockSpec(memory_space=pltpu.VMEM),
            scratch_shapes=[
                pltpu.VMEM((samples, width), jnp.bfloat16),
                pltpu.VMEM((samples, width), jnp.bfloat16),
                pltpu.VMEM((steps, B, B), jnp.float32),
                sent,
                sent,
                sent,
                sent,
                pltpu.SemaphoreType.DMA((rows,)),
                pltpu.SemaphoreType.DMA((rows,)),
                pltpu.SemaphoreType.DMA((rows,)),
                pltpu.SemaphoreType.DMA((steps,)),
                pltpu.SemaphoreType.DMA((steps,)),
                pltpu.SemaphoreType.DMA((steps,)),
                pltpu.SemaphoreType.DMA((steps,)),
            ],
            compiler_params=pltpu.CompilerParams(
                collective_id=0,
                has_side_effects=True,
                vmem_limit_bytes=63 * 1024 * 1024,
            ),
        )(genotypes)

    return jax.shard_map(
        per_device,
        mesh=mesh,
        in_specs=(P(None, ("slab", "genome", "group")),),
        out_specs=P(("slab", "genome", "group")),
        check_vma=False,
    )
```

time: 27.9 us -> 29.7 us (1.065)
  the two profiles are of different devices: /device:TPU:1 before, /device:TPU:0 now
where the time goes in v2:
time: 29.7 us; the launch traced here: 29.5 us
  Pallas kernels  28.2 us (95%)
  local copies, waits for them, and re-layouts  1.26 us (4%)
    pallas_call x1, Pallas kernels, per_device(): pl.pallas_call(functools.partial(kernel, n, ng), out_shape=jax.ShapeDtype...  28.2 us
    unnamed x1, local copies, waits for them, and re-layouts  1.26 us

profile of v2, /device:TPU:0, one launch (start us, length us, event | category | flops | bytes accessed | tf_op | source)
XLA Modules:
  0.0 29.5 jit_solution(7779736901004238747)
XLA Ops:
  0.0 28.2 %shard_map.17 = f32[384]{0:T(512)} custom-call(bf16[640,384]{1,0:T(8,128)(2,1)} %given.1), custom_call_target="tpu_custom_call" | custom-call | tf_op jit(solution)/shard_map/pallas_call | solution.py:211
  28.3 1.3 %copy.3 = f32[384]{0:T(512)} copy(f32[384]{0:T(512)} %shard_map.17) | data formatting | bytes 3072

commit v3 on v2

v3 whole, which is shorter than its diff:
```python
import functools

import jax
import jax.numpy as jnp
from jax import lax
from jax.experimental import pallas as pl
from jax.experimental.pallas import tpu as pltpu
from jax.sharding import PartitionSpec as P

MESH = pl.DeviceIdType.MESH
B = 128
SKEW = 3
LAG = 3


def triangle(rows):
    return [(i, j) for i in range(rows) for j in range(i + 1)]


def kernel(
    n, ng, given, out, mine, following, own, from_left, from_right, to_right, to_left,
    from_next, to_before, m_sem, x_send, x_recv, s_send, s_recv, r_send, r_recv, l_send, l_recv,
):
    z = lax.axis_index("group")
    g = lax.axis_index("genome")
    samples, width = given.shape
    rows = samples // B
    blocks = triangle(rows)
    first = [i * (i + 1) // 2 for i in range(rows)]
    late = rows - 1

    has_left, has_right = z > 0, z < n - 1
    has_before, has_next = g > 0, g < ng - 1

    barrier = pltpu.get_barrier_semaphore()

    def greet(there, where):
        @pl.when(there)
        def _():
            pl.semaphore_signal(barrier, inc=1, device_id=where, device_id_type=MESH)

    greet(has_left, {"group": z - 1})
    greet(has_right, {"group": z + 1})
    greet(has_next, {"genome": g + 1})
    def load(i):
        span = pl.ds(i * B, B)
        return pltpu.make_async_copy(given.at[span], mine.at[span], m_sem.at[i])

    for i in range(rows):
        load(i).start()

    peers = jnp.minimum(z, 1) + jnp.minimum(n - 1 - z, 1) + jnp.minimum(g, 1)
    pl.semaphore_wait(barrier, peers)

    def slice_copy():
        return pltpu.make_async_remote_copy(
            src_ref=mine,
            dst_ref=following,
            send_sem=x_send,
            recv_sem=x_recv,
            device_id={"genome": g - 1},
            device_id_type=MESH,
        )

    def sum_copy(c):
        return pltpu.make_async_remote_copy(
            src_ref=to_before.at[c],
            dst_ref=from_next.at[c],
            send_sem=s_send.at[c],
            recv_sem=s_recv.at[c],
            device_id={"genome": g - 1},
            device_id_type=MESH,
        )

    def right_copy(c):
        return pltpu.make_async_remote_copy(
            src_ref=to_right.at[c],
            dst_ref=from_left.at[c],
            send_sem=r_send.at[c],
            recv_sem=r_recv.at[c],
            device_id={"group": z + 1},
            device_id_type=MESH,
        )

    def left_copy(c):
        return pltpu.make_async_remote_copy(
            src_ref=to_left.at[c],
            dst_ref=from_right.at[c],
            send_sem=l_send.at[c],
            recv_sem=l_recv.at[c],
            device_id={"group": z - 1},
            device_id_type=MESH,
        )

    def products(ref, i, add):
        band = lax.dot_general(
            ref[pl.ds(i * B, B), :],
            ref[pl.ds(0, (i + 1) * B), :],
            (((1,), (1,)), ((), ())),
            preferred_element_type=jnp.float32,
        )
        for j in range(i + 1):
            block = band[:, j * B : (j + 1) * B]
            own[first[i] + j] = own[first[i] + j] + block if add else block

    score = jnp.zeros((1, width), jnp.float32)

    def scored(score, i):
        span = pl.ds(first[i], i + 1)
        if i < late:

            @pl.when(has_next)
            def _():
                for j in range(i + 1):
                    sum_copy(first[i] + j).wait_recv()
                own[span] = own[span] + from_next[span].astype(jnp.float32)

        parts = []
        for j in range(i + 1):
            part = own[first[i] + j]
            parts.append(part if j == i else part + part)
        whole = jnp.concatenate(parts, axis=1) if i else parts[0]
        high = whole.astype(jnp.bfloat16)
        low = (whole - high.astype(jnp.float32)).astype(jnp.bfloat16)
        both = lax.dot_general(
            jnp.concatenate([high, low], axis=0),
            mine[pl.ds(0, (i + 1) * B), :],
            (((1,), (0,)), ((), ())),
            preferred_element_type=jnp.float32,
        )
        weighed = both[:B] + both[B:]
        return score + jnp.sum(
            weighed * mine[pl.ds(i * B, B), :].astype(jnp.float32),
            axis=0,
            keepdims=True,
        )

    load(0).wait()
    products(mine, 0, False)

    for t in range(len(blocks) + SKEW * (n - 1)):
        if t == first[late]:

            @pl.when(has_next)
            def _():
                slice_copy().wait_recv()
                products(following, late, True)

        c = t - SKEW * z

        @pl.when(has_right & (c >= 0) & (c < len(blocks)))
        def _():
            @pl.when(has_left)
            def _():
                right_copy(c).wait_recv()
                total = own[c] + from_left[c].astype(jnp.float32)
                to_right[c] = total.astype(to_right.dtype)

            @pl.when(z == 0)
            def _():
                to_right[c] = own[c].astype(to_right.dtype)

            right_copy(c).start()

        d = t - SKEW * (n - 1 - z)

        @pl.when(has_left & (d >= 0) & (d < len(blocks)))
        def _():
            @pl.when(has_right)
            def _():
                left_copy(d).wait_recv()
                total = own[d] + from_right[d].astype(jnp.float32)
                to_left[d] = total.astype(to_left.dtype)

            @pl.when(z == n - 1)
            def _():
                to_left[d] = own[d].astype(to_left.dtype)

            left_copy(d).start()

        if t == 0:
            for i in range(1, rows):
                load(i).wait()

            @pl.when(has_before)
            def _():
                slice_copy().start()

        if t in first[: rows - 1]:
            products(mine, first.index(t) + 1, False)

        f = t - SKEW * jnp.maximum(z, n - 1 - z)

        @pl.when((f >= 0) & (f < len(blocks)))
        def _():
            @pl.when(has_left)
            def _():
                @pl.when(z == n - 1)
                def _():
                    right_copy(f).wait_recv()

                own[f] = own[f] + from_left[f].astype(jnp.float32)

            @pl.when(has_right)
            def _():
                @pl.when(z == 0)
                def _():
                    left_copy(f).wait_recv()

                own[f] = own[f] + from_right[f].astype(jnp.float32)

            @pl.when(has_before & (f < first[late]))
            def _():
                to_before[f] = own[f].astype(to_before.dtype)
                sum_copy(f).start()

        ready = t - LAG - SKEW * (n - 1)
        for i in range(late):
            if ready == first[i] + i:
                score = scored(score, i)

    for i in range(late, rows):
        score = scored(score, i)
    out[...] = score * (1.0 / samples) * (1.0 / samples)

    @pl.when(has_before)
    def _():
        slice_copy().wait_send()
        for c in range(first[late]):
            sum_copy(c).wait_send()

    @pl.when(has_right)
    def _():
        for c in range(len(blocks)):
            right_copy(c).wait_send()

    @pl.when(has_left)
    def _():
        for c in range(len(blocks)):
            left_copy(c).wait_send()


def solution(mesh):
    n, ng = mesh.shape["group"], mesh.shape["genome"]

    def per_device(genotypes):
        samples, width = genotypes.shape
        rows = samples // B
        steps = len(triangle(rows))
        sent = pltpu.VMEM((steps, B, B), jnp.bfloat16)
        scores = pl.pallas_call(
            functools.partial(kernel, n, ng),
            out_shape=jax.ShapeDtypeStruct((1, width), jnp.float32),
            in_specs=[pl.BlockSpec(memory_space=pl.ANY)],
            out_specs=pl.BlockSpec(memory_space=pltpu.VMEM),
            scratch_shapes=[
                pltpu.VMEM((samples, width), jnp.bfloat16),
                pltpu.VMEM((samples, width), jnp.bfloat16),
                pltpu.VMEM((steps, B, B), jnp.float32),
                sent,
                sent,
                sent,
                sent,
                sent,
                sent,
                pltpu.SemaphoreType.DMA((rows,)),
                pltpu.SemaphoreType.DMA,
                pltpu.SemaphoreType.DMA,
                pltpu.SemaphoreType.DMA((steps,)),
                pltpu.SemaphoreType.DMA((steps,)),
                pltpu.SemaphoreType.DMA((steps,)),
                pltpu.SemaphoreType.DMA((steps,)),
                pltpu.SemaphoreType.DMA((steps,)),
                pltpu.SemaphoreType.DMA((steps,)),
            ],
            compiler_params=pltpu.CompilerParams(
                collective_id=0,
                has_side_effects=True,
                vmem_limit_bytes=63 * 1024 * 1024,
            ),
        )(genotypes)
        return scores.reshape(width)

    return jax.shard_map(
        per_device,
        mesh=mesh,
        in_specs=(P(None, ("slab", "genome", "group")),),
        out_specs=P(("slab", "genome", "group")),
        check_vma=False,
    )
```

time: 29.7 us -> 29.2 us (0.983)
  other arithmetic: 0 us -> 1.28 us
  local copies, waits for them, and re-layouts: 1.26 us -> 0 us
  Pallas kernels: 28.2 us -> 27.7 us
    pallas_call x0 -> x1, other arithmetic: none -> 1.28 us  [per_device(): pl.pallas_call(functools.partial(kernel, n, ng), out_shape=jax.ShapeDtype...]
    unnamed x1 -> x0, local copies, waits for them, and re-layouts: 1.26 us -> none
    pallas_call x1, Pallas kernels: 28.2 us -> 27.7 us  [per_device(): pl.pallas_call(functools.partial(kernel, n, ng), out_shape=jax.ShapeDtype...]
where the time goes in v3:
time: 29.2 us; the launch traced here: 29 us
  Pallas kernels  27.7 us (95%)
  other arithmetic  1.28 us (4%)
    pallas_call x1, Pallas kernels, per_device(): pl.pallas_call(functools.partial(kernel, n, ng), out_shape=jax.ShapeDtype...  27.7 us
    pallas_call x1, other arithmetic, per_device(): pl.pallas_call(functools.partial(kernel, n, ng), out_shape=jax.ShapeDtype...  1.28 us

profile of v3, /device:TPU:0, one launch (start us, length us, event | category | flops | bytes accessed | tf_op | source)
XLA Modules:
  0.0 29.0 jit_solution(523324010950778893)
XLA Ops:
  0.0 27.7 %shard_map.17 = f32[1,384]{1,0:T(1,128)} custom-call(bf16[640,384]{1,0:T(8,128)(2,1)} %given.1), custom_call_target="tpu_custom_call" | custom-call | tf_op jit(solution)/shard_map/pallas_call | solution.py:251
  27.8 1.3 %reduce = f32[384]{0:T(512)} reduce(f32[1,384]{1,0:T(1,128)} %shard_map.17, f32[]{:T(128)} %constant), dimensions={0}, to_apply=%pallas_call.3.reduce_sub_computation | reduce | bytes 3076 | tf_op jit(solution)/shard_map/pallas_call | solution.py:251

commit v4 on v1

v4 whole, which is shorter than its diff:
```python
import functools

import jax
import jax.numpy as jnp
from jax import lax
from jax.experimental import pallas as pl
from jax.experimental.pallas import tpu as pltpu
from jax.sharding import PartitionSpec as P

MESH = pl.DeviceIdType.MESH
B = 128
SKEW = 2
LAG = 1


def plan(samples):
    blocks = [(i, j) for i in range(samples // B) for j in range(i + 1)]
    per = 3 if len(blocks) % 3 == 0 else 1
    chunks = [list(range(k, k + per)) for k in range(0, len(blocks), per)]
    return blocks, per, chunks


def pieces(blocks, chunk):
    runs = []
    for b in chunk:
        i, j = blocks[b]
        if runs and runs[-1][0] == i:
            runs[-1][3] += 1
        else:
            runs.append([i, j, b, 1])
    return runs


def kernel(
    n, ng, given, out, mine, own, from_left, from_right, to_right, to_left,
    from_next, to_before, m_sem, s_send, s_recv, r_send, r_recv, l_send, l_recv,
):
    z = lax.axis_index("group")
    g = lax.axis_index("genome")
    samples, width = given.shape
    rows = samples // B
    blocks, per, chunks = plan(samples)
    steps = len(chunks)

    has_left, has_right = z > 0, z < n - 1
    has_before, has_next = g > 0, g < ng - 1

    barrier = pltpu.get_barrier_semaphore()

    def greet(there, where):
        @pl.when(there)
        def _():
            pl.semaphore_signal(barrier, inc=1, device_id=where, device_id_type=MESH)

    greet(has_left, {"group": z - 1})
    greet(has_right, {"group": z + 1})
    greet(has_next, {"genome": g + 1})
    def load(i):
        span = pl.ds(i * B, B)
        return pltpu.make_async_copy(given.at[span], mine.at[span], m_sem.at[i])

    for i in range(rows):
        load(i).start()

    peers = jnp.minimum(z, 1) + jnp.minimum(n - 1 - z, 1) + jnp.minimum(g, 1)
    pl.semaphore_wait(barrier, peers)

    def sum_copy(c):
        return pltpu.make_async_remote_copy(
            src_ref=to_before.at[pl.ds(c * per, per)],
            dst_ref=from_next.at[pl.ds(c * per, per)],
            send_sem=s_send.at[c],
            recv_sem=s_recv.at[c],
            device_id={"genome": g - 1},
            device_id_type=MESH,
        )

    def right_copy(c):
        return pltpu.make_async_remote_copy(
            src_ref=to_right.at[pl.ds(c * per, per)],
            dst_ref=from_left.at[pl.ds(c * per, per)],
            send_sem=r_send.at[c],
            recv_sem=r_recv.at[c],
            device_id={"group": z + 1},
            device_id_type=MESH,
        )

    def left_copy(c):
        return pltpu.make_async_remote_copy(
            src_ref=to_left.at[pl.ds(c * per, per)],
            dst_ref=from_right.at[pl.ds(c * per, per)],
            send_sem=l_send.at[c],
            recv_sem=l_recv.at[c],
            device_id={"group": z - 1},
            device_id_type=MESH,
        )

    def products(chunk):
        for i, j, b, count in pieces(blocks, chunk):
            band = lax.dot_general(
                mine[pl.ds(i * B, B), :],
                mine[pl.ds(j * B, count * B), :],
                (((1,), (1,)), ((), ())),
                preferred_element_type=jnp.float32,
            )
            for k in range(count):
                own[b + k] = band[:, k * B : (k + 1) * B]

    def scored(score, c):
        span = pl.ds(c * per, per)

        @pl.when(has_next)
        def _():
            sum_copy(c).wait_recv()
            own[span] = own[span] + from_next[span].astype(jnp.float32)

        for i, j, b, count in pieces(blocks, chunks[c]):
            parts = []
            for k in range(count):
                part = own[b + k]
                parts.append(part if j + k == i else part + part)
            whole = jnp.concatenate(parts, axis=1) if count > 1 else parts[0]
            high = whole.astype(jnp.bfloat16)
            low = (whole - high.astype(jnp.float32)).astype(jnp.bfloat16)
            both = lax.dot_general(
                jnp.concatenate([high, low], axis=0),
                mine[pl.ds(j * B, count * B), :],
                (((1,), (0,)), ((), ())),
                preferred_element_type=jnp.float32,
            )
            weighed = both[:B] + both[B:]
            score = score + jnp.sum(
                weighed * mine[pl.ds(i * B, B), :].astype(jnp.float32),
                axis=0,
                keepdims=True,
            )
        return score

    score = jnp.zeros((1, width), jnp.float32)
    loaded = 0
    for t in range(-1, steps + SKEW * (n - 1)):
        c = t - SKEW * z

        @pl.when(has_right & (c >= 0) & (c < steps))
        def _():
            span = pl.ds(c * per, per)

            @pl.when(has_left)
            def _():
                right_copy(c).wait_recv()
                total = own[span] + from_left[span].astype(jnp.float32)
                to_right[span] = total.astype(to_right.dtype)

            @pl.when(z == 0)
            def _():
                to_right[span] = own[span].astype(to_right.dtype)

            right_copy(c).start()

        d = t - SKEW * (n - 1 - z)

        @pl.when(has_left & (d >= 0) & (d < steps))
        def _():
            span = pl.ds(d * per, per)

            @pl.when(has_right)
            def _():
                left_copy(d).wait_recv()
                total = own[span] + from_right[span].astype(jnp.float32)
                to_left[span] = total.astype(to_left.dtype)

            @pl.when(z == n - 1)
            def _():
                to_left[span] = own[span].astype(to_left.dtype)

            left_copy(d).start()

        if t + 1 < steps:
            need = blocks[chunks[t + 1][-1]][0] + 1
            for i in range(loaded, need):
                load(i).wait()
            loaded = need
            products(chunks[t + 1])

        f = t - SKEW * jnp.maximum(z, n - 1 - z)

        @pl.when((f >= 0) & (f < steps))
        def _():
            span = pl.ds(f * per, per)

            @pl.when(has_left)
            def _():
                @pl.when(z == n - 1)
                def _():
                    right_copy(f).wait_recv()

                own[span] = own[span] + from_left[span].astype(jnp.float32)

            @pl.when(has_right)
            def _():
                @pl.when(z == 0)
                def _():
                    left_copy(f).wait_recv()

                own[span] = own[span] + from_right[span].astype(jnp.float32)

            @pl.when(has_before)
            def _():
                to_before[span] = own[span].astype(to_before.dtype)
                sum_copy(f).start()

        ready = t - LAG - SKEW * (n - 1)
        if ready >= 0:
            score = scored(score, ready)

    for c in range(steps - LAG, steps):
        score = scored(score, c)
    out[...] = score * (1.0 / samples) * (1.0 / samples)

    @pl.when(has_before)
    def _():
        for c in range(steps):
            sum_copy(c).wait_send()

    @pl.when(has_right)
    def _():
        for c in range(steps):
            right_copy(c).wait_send()

    @pl.when(has_left)
    def _():
        for c in range(steps):
            left_copy(c).wait_send()


def solution(mesh):
    n, ng = mesh.shape["group"], mesh.shape["genome"]

    def per_device(genotypes):
        samples, width = genotypes.shape
        blocks, per, chunks = plan(samples)
        steps = len(chunks)
        sent = pltpu.VMEM((len(blocks), B, B), jnp.bfloat16)
        scores = pl.pallas_call(
            functools.partial(kernel, n, ng),
            out_shape=jax.ShapeDtypeStruct((1, width), jnp.float32),
            in_specs=[pl.BlockSpec(memory_space=pl.ANY)],
            out_specs=pl.BlockSpec(memory_space=pltpu.VMEM),
            scratch_shapes=[
                pltpu.VMEM((samples, width), jnp.bfloat16),
                pltpu.VMEM((len(blocks), B, B), jnp.float32),
                sent,
                sent,
                sent,
                sent,
                sent,
                sent,
                pltpu.SemaphoreType.DMA((samples // B,)),
                pltpu.SemaphoreType.DMA((steps,)),
                pltpu.SemaphoreType.DMA((steps,)),
                pltpu.SemaphoreType.DMA((steps,)),
                pltpu.SemaphoreType.DMA((steps,)),
                pltpu.SemaphoreType.DMA((steps,)),
                pltpu.SemaphoreType.DMA((steps,)),
            ],
            compiler_params=pltpu.CompilerParams(
                collective_id=0,
                has_side_effects=True,
                vmem_limit_bytes=63 * 1024 * 1024,
            ),
        )(genotypes)
        return scores.reshape(width)

    return jax.shard_map(
        per_device,
        mesh=mesh,
        in_specs=(P(None, ("slab", "genome", "group")),),
        out_specs=P(("slab", "genome", "group")),
        check_vma=False,
    )
```

time: 27.9 us -> 31.1 us (1.11)
  Pallas kernels: 26.1 us -> 29.6 us
  local copies, waits for them, and re-layouts: 1.03 us -> 0 us
  other arithmetic: 0.6 us -> 1.28 us
    pallas_call x1, Pallas kernels: 26.1 us -> 29.6 us  [per_device(): pl.pallas_call(functools.partial(kernel, n, ng), out_shape=jax.ShapeDtype...]
    unnamed x2 -> x0, local copies, waits for them, and re-layouts: 1.03 us -> none
    pallas_call x1, other arithmetic: 0.6 us -> 1.28 us  [per_device(): pl.pallas_call(functools.partial(kernel, n, ng), out_shape=jax.ShapeDtype...]
where the time goes in v4:
time: 31.1 us; the launch traced here: 30.9 us
  Pallas kernels  29.6 us (95%)
  other arithmetic  1.28 us (4%)
    pallas_call x1, Pallas kernels, per_device(): pl.pallas_call(functools.partial(kernel, n, ng), out_shape=jax.ShapeDtype...  29.6 us
    pallas_call x1, other arithmetic, per_device(): pl.pallas_call(functools.partial(kernel, n, ng), out_shape=jax.ShapeDtype...  1.28 us

profile of v4, /device:TPU:1, one launch (start us, length us, event | category | flops | bytes accessed | tf_op | source)
XLA Modules:
  0.0 30.9 jit_solution(10931385620259295470)
XLA Ops:
  0.0 29.6 %shard_map.17 = f32[1,384]{1,0:T(1,128)} custom-call(bf16[640,384]{1,0:T(8,128)(2,1)} %given.1), custom_call_target="tpu_custom_call" | custom-call | tf_op jit(solution)/shard_map/pallas_call | solution.py:244
  29.7 1.3 %reduce = f32[384]{0:T(512)} reduce(f32[1,384]{1,0:T(1,128)} %shard_map.17, f32[]{:T(128)} %constant), dimensions={0}, to_apply=%pallas_call.3.reduce_sub_computation | reduce | bytes 3076 | tf_op jit(solution)/shard_map/pallas_call | solution.py:244

commit v5 on v3

--- a/solution.py
+++ b/solution.py
@@ -10,7 +10,7 @@
 MESH = pl.DeviceIdType.MESH
 B = 128
 SKEW = 3
-LAG = 3
+LAG = 6
 
 
 def triangle(rows):
@@ -52,12 +52,13 @@
     peers = jnp.minimum(z, 1) + jnp.minimum(n - 1 - z, 1) + jnp.minimum(g, 1)
     pl.semaphore_wait(barrier, peers)
 
-    def slice_copy():
-        return pltpu.make_async_remote_copy(
-            src_ref=mine,
-            dst_ref=following,
-            send_sem=x_send,
-            recv_sem=x_recv,
+    def row_copy(i):
+        span = pl.ds(i * B, B)
+        return pltpu.make_async_remote_copy(
+            src_ref=mine.at[span],
+            dst_ref=following.at[span],
+            send_sem=x_send.at[i],
+            recv_sem=x_recv.at[i],
             device_id={"genome": g - 1},
             device_id_type=MESH,
         )
@@ -135,15 +136,24 @@
             keepdims=True,
         )
 
-    load(0).wait()
+    for i in range(rows):
+        load(i).wait()
+
+    @pl.when(has_before)
+    def _():
+        for i in range(rows):
+            row_copy(i).start()
+
     products(mine, 0, False)
+    pending = list(range(rows))
 
     for t in range(len(blocks) + SKEW * (n - 1)):
         if t == first[late]:
 
             @pl.when(has_next)
             def _():
-                slice_copy().wait_recv()
+                for i in range(rows):
+                    row_copy(i).wait_recv()
                 products(following, late, True)
 
         c = t - SKEW * z
@@ -178,14 +188,6 @@
 
             left_copy(d).start()
 
-        if t == 0:
-            for i in range(1, rows):
-                load(i).wait()
-
-            @pl.when(has_before)
-            def _():
-                slice_copy().start()
-
         if t in first[: rows - 1]:
             products(mine, first.index(t) + 1, False)
 
@@ -215,17 +217,17 @@
                 sum_copy(f).start()
 
         ready = t - LAG - SKEW * (n - 1)
-        for i in range(late):
-            if ready == first[i] + i:
-                score = scored(score, i)
-
-    for i in range(late, rows):
+        if pending[0] < late and ready == first[pending[0]] + pending[0]:
+            score = scored(score, pending.pop(0))
+
+    for i in pending:
         score = scored(score, i)
     out[...] = score * (1.0 / samples) * (1.0 / samples)
 
     @pl.when(has_before)
     def _():
-        slice_copy().wait_send()
+        for i in range(rows):
+            row_copy(i).wait_send()
         for c in range(first[late]):
             sum_copy(c).wait_send()
 
@@ -264,8 +266,8 @@
                 sent,
                 sent,
                 pltpu.SemaphoreType.DMA((rows,)),
-                pltpu.SemaphoreType.DMA,
-                pltpu.SemaphoreType.DMA,
+                pltpu.SemaphoreType.DMA((rows,)),
+                pltpu.SemaphoreType.DMA((rows,)),
                 pltpu.SemaphoreType.DMA((steps,)),
                 pltpu.SemaphoreType.DMA((steps,)),
                 pltpu.SemaphoreType.DMA((steps,)),

time: 29.2 us -> 29.9 us (1.024)
  Pallas kernels: 27.7 us -> 28.5 us
    pallas_call x1, Pallas kernels: 27.7 us -> 28.5 us  [per_device(): pl.pallas_call(functools.partial(kernel, n, ng), out_shape=jax.ShapeDtype...]
where the time goes in v5:
time: 29.9 us; the launch traced here: 29.8 us
  Pallas kernels  28.5 us (95%)
  other arithmetic  1.28 us (4%)
    pallas_call x1, Pallas kernels, per_device(): pl.pallas_call(functools.partial(kernel, n, ng), out_shape=jax.ShapeDtype...  28.5 us
    pallas_call x1, other arithmetic, per_device(): pl.pallas_call(functools.partial(kernel, n, ng), out_shape=jax.ShapeDtype...  1.28 us

profile of v5, /device:TPU:0, one launch (start us, length us, event | category | flops | bytes accessed | tf_op | source)
XLA Modules:
  0.0 29.8 jit_solution(12522498063004554501)
XLA Ops:
  0.0 28.5 %shard_map.17 = f32[1,384]{1,0:T(1,128)} custom-call(bf16[640,384]{1,0:T(8,128)(2,1)} %given.1), custom_call_target="tpu_custom_call" | custom-call | tf_op jit(solution)/shard_map/pallas_call | solution.py:253
  28.5 1.3 %reduce = f32[384]{0:T(512)} reduce(f32[1,384]{1,0:T(1,128)} %shard_map.17, f32[]{:T(128)} %constant), dimensions={0}, to_apply=%pallas_call.3.reduce_sub_computation | reduce | bytes 3076 | tf_op jit(solution)/shard_map/pallas_call | solution.py:253

commit v6 on v5

v6 whole, which is shorter than its diff:
```python
import functools

import jax
import jax.numpy as jnp
from jax import lax
from jax.experimental import pallas as pl
from jax.experimental.pallas import tpu as pltpu
from jax.sharding import PartitionSpec as P

MESH = pl.DeviceIdType.MESH
B = 128
SKEW = 4


def triangle(rows):
    return [(i, j) for i in range(rows) for j in range(i + 1)]


def kernel(
    n, ng, given, out, mine, before, own, from_left, from_right, to_right, to_left,
    kept, to_before, from_next, m_sem, x_send, x_recv, s_send, s_recv,
    r_send, r_recv, l_send, l_recv,
):
    z = lax.axis_index("group")
    g = lax.axis_index("genome")
    samples, width = given.shape
    rows = samples // B
    blocks = triangle(rows)
    first = [i * (i + 1) // 2 for i in range(rows)]
    groups = [(i, 0, i + 1) for i in range(rows - 1)]
    groups += [(rows - 1, 0, rows - 2), (rows - 1, rows - 2, 2)]

    has_left, has_right = z > 0, z < n - 1
    has_before, has_next = g > 0, g < ng - 1

    barrier = pltpu.get_barrier_semaphore()

    def greet(there, where):
        @pl.when(there)
        def _():
            pl.semaphore_signal(barrier, inc=1, device_id=where, device_id_type=MESH)

    greet(has_left, {"group": z - 1})
    greet(has_right, {"group": z + 1})
    greet(has_before, {"genome": g - 1})
    greet(has_next, {"genome": g + 1})

    def load(i):
        span = pl.ds(i * B, B)
        return pltpu.make_async_copy(given.at[span], mine.at[span], m_sem.at[i])

    for i in range(rows):
        load(i).start()

    peers = jnp.minimum(z, 1) + jnp.minimum(n - 1 - z, 1)
    peers = peers + jnp.minimum(g, 1) + jnp.minimum(ng - 1 - g, 1)
    pl.semaphore_wait(barrier, peers)

    def row_copy(i):
        span = pl.ds(i * B, B)
        return pltpu.make_async_remote_copy(
            src_ref=mine.at[span],
            dst_ref=before.at[span],
            send_sem=x_send.at[i],
            recv_sem=x_recv.at[i],
            device_id={"genome": g + 1},
            device_id_type=MESH,
        )

    def score_copy():
        return pltpu.make_async_remote_copy(
            src_ref=to_before,
            dst_ref=from_next,
            send_sem=s_send,
            recv_sem=s_recv,
            device_id={"genome": g - 1},
            device_id_type=MESH,
        )

    def right_copy(c):
        return pltpu.make_async_remote_copy(
            src_ref=to_right.at[c],
            dst_ref=from_left.at[c],
            send_sem=r_send.at[c],
            recv_sem=r_recv.at[c],
            device_id={"group": z + 1},
            device_id_type=MESH,
        )

    def left_copy(c):
        return pltpu.make_async_remote_copy(
            src_ref=to_left.at[c],
            dst_ref=from_right.at[c],
            send_sem=l_send.at[c],
            recv_sem=l_recv.at[c],
            device_id={"group": z - 1},
            device_id_type=MESH,
        )

    def products(i):
        band = lax.dot_general(
            mine[pl.ds(i * B, B), :],
            mine[pl.ds(0, (i + 1) * B), :],
            (((1,), (1,)), ((), ())),
            preferred_element_type=jnp.float32,
        )
        for j in range(i + 1):
            own[first[i] + j] = band[:, j * B : (j + 1) * B]

    def scored(group):
        i, j, count = group
        parts = []
        for k in range(j, j + count):
            part = own[first[i] + k]
            parts.append(part if k == i else part + part)
        whole = jnp.concatenate(parts, axis=1) if count > 1 else parts[0]
        high = whole.astype(jnp.bfloat16)
        low = (whole - high.astype(jnp.float32)).astype(jnp.bfloat16)
        both = jnp.concatenate([high, low], axis=0)

        def add(total, ref):
            product = lax.dot_general(
                both,
                ref[pl.ds(j * B, count * B), :],
                (((1,), (0,)), ((), ())),
                preferred_element_type=jnp.float32,
            )
            weighed = (product[:B] + product[B:]) * ref[pl.ds(i * B, B), :].astype(
                jnp.float32
            )
            total[...] += jnp.sum(weighed, axis=0, keepdims=True)

        @pl.when(has_before)
        def _():
            if group == groups[0]:
                for k in range(rows):
                    row_copy(k).wait_recv()
            add(to_before, before)

        add(kept, mine)

    for i in range(rows):
        load(i).wait()

    products(0)
    kept[...] = jnp.zeros_like(kept)
    to_before[...] = jnp.zeros_like(to_before)
    pending = list(groups)
    at_end = (z == 0) | (z == n - 1)

    for t in range(len(blocks) + SKEW * (n - 1)):
        c = t - SKEW * z

        @pl.when(has_right & (c >= 0) & (c < len(blocks)))
        def _():
            @pl.when(has_left)
            def _():
                right_copy(c).wait_recv()
                total = own[c] + from_left[c].astype(jnp.float32)
                to_right[c] = total.astype(to_right.dtype)

            @pl.when(z == 0)
            def _():
                to_right[c] = own[c].astype(to_right.dtype)

            right_copy(c).start()

        d = t - SKEW * (n - 1 - z)

        @pl.when(has_left & (d >= 0) & (d < len(blocks)))
        def _():
            @pl.when(has_right)
            def _():
                left_copy(d).wait_recv()
                total = own[d] + from_right[d].astype(jnp.float32)
                to_left[d] = total.astype(to_left.dtype)

            @pl.when(z == n - 1)
            def _():
                to_left[d] = own[d].astype(to_left.dtype)

            left_copy(d).start()

        if t in first[: rows - 1]:
            products(first.index(t) + 1)

        if t == 1:

            @pl.when(has_next)
            def _():
                for i in range(rows):
                    row_copy(i).start()

        f = t - SKEW * jnp.maximum(z, n - 1 - z)

        @pl.when((f >= 0) & (f < len(blocks)))
        def _():
            @pl.when(has_left)
            def _():
                @pl.when(z == n - 1)
                def _():
                    right_copy(f).wait_recv()

                own[f] = own[f] + from_left[f].astype(jnp.float32)

            @pl.when(has_right)
            def _():
                @pl.when(z == 0)
                def _():
                    left_copy(f).wait_recv()

                own[f] = own[f] + from_right[f].astype(jnp.float32)

        ready = t - SKEW * (n - 1)
        group = pending[0]
        if ready == first[group[0]] + group[1] + group[2] - 1:

            @pl.when(at_end)
            def _():
                scored(group)

            pending.pop(0)

    @pl.when(jnp.logical_not(at_end))
    def _():
        for group in groups:
            scored(group)

    @pl.when(has_before)
    def _():
        score_copy().start()

    @pl.when(has_next)
    def _():
        score_copy().wait_recv()
        kept[...] += from_next[...]

    out[...] = kept[...] * (1.0 / samples) * (1.0 / samples)

    @pl.when(has_next)
    def _():
        for i in range(rows):
            row_copy(i).wait_send()

    @pl.when(has_before)
    def _():
        score_copy().wait_send()

    @pl.when(has_right)
    def _():
        for c in range(len(blocks)):
            right_copy(c).wait_send()

    @pl.when(has_left)
    def _():
        for c in range(len(blocks)):
            left_copy(c).wait_send()


def solution(mesh):
    n, ng = mesh.shape["group"], mesh.shape["genome"]

    def per_device(genotypes):
        samples, width = genotypes.shape
        rows = samples // B
        steps = len(triangle(rows))
        sent = pltpu.VMEM((steps, B, B), jnp.bfloat16)
        line = pltpu.VMEM((1, width), jnp.float32)
        scores = pl.pallas_call(
            functools.partial(kernel, n, ng),
            out_shape=jax.ShapeDtypeStruct((1, width), jnp.float32),
            in_specs=[pl.BlockSpec(memory_space=pl.ANY)],
            out_specs=pl.BlockSpec(memory_space=pltpu.VMEM),
            scratch_shapes=[
                pltpu.VMEM((samples, width), jnp.bfloat16),
                pltpu.VMEM((samples, width), jnp.bfloat16),
                pltpu.VMEM((steps, B, B), jnp.float32),
                sent,
                sent,
                sent,
                sent,
                line,
                line,
                line,
                pltpu.SemaphoreType.DMA((rows,)),
                pltpu.SemaphoreType.DMA((rows,)),
                pltpu.SemaphoreType.DMA((rows,)),
                pltpu.SemaphoreType.DMA,
                pltpu.SemaphoreType.DMA,
                pltpu.SemaphoreType.DMA((steps,)),
                pltpu.SemaphoreType.DMA((steps,)),
                pltpu.SemaphoreType.DMA((steps,)),
                pltpu.SemaphoreType.DMA((steps,)),
            ],
            compiler_params=pltpu.CompilerParams(
                collective_id=0,
                has_side_effects=True,
                vmem_limit_bytes=54784 * 1024,
            ),
        )(genotypes)
        return scores.reshape(width)

    return jax.shard_map(
        per_device,
        mesh=mesh,
        in_specs=(P(None, ("slab", "genome", "group")),),
        out_specs=P(("slab", "genome", "group")),
        check_vma=False,
    )
```

time: 29.9 us -> 27.8 us (0.930)
  the two profiles are of different devices: /device:TPU:0 before, /device:TPU:1 now
where the time goes in v6:
time: 27.8 us; the launch traced here: 27.7 us
  Pallas kernels  27.1 us (97%)
  other arithmetic  0.6 us (2%)
    pallas_call x1, Pallas kernels, per_device(): pl.pallas_call(functools.partial(kernel, n, ng), out_shape=jax.ShapeDtype...  27.1 us
    pallas_call x1, other arithmetic, per_device(): pl.pallas_call(functools.partial(kernel, n, ng), out_shape=jax.ShapeDtype...  0.6 us

profile of v6, /device:TPU:1, one launch (start us, length us, event | category | flops | bytes accessed | tf_op | source)
XLA Modules:
  0.0 27.7 jit_solution(10785885391000061003)
XLA Ops:
  0.0 27.1 %shard_map.17 = f32[1,384]{1,0:T(1,128)S(1)} custom-call(bf16[640,384]{1,0:T(8,128)(2,1)} %given.1), custom_call_target="tpu_custom_call" | custom-call | tf_op jit(solution)/shard_map/pallas_call | solution.py:269
  27.1 0.6 %reduce = f32[384]{0:T(512)} reduce(f32[1,384]{1,0:T(1,128)S(1)} %shard_map.17, f32[]{:T(128)} %constant), dimensions={0}, to_apply=%pallas_call.3.reduce_sub_computation | reduce | bytes 3076 | tf_op jit(solution)/shard_map/pallas_call | solution.py:269

commit v7 on v6

--- a/solution.py
+++ b/solution.py
@@ -17,8 +17,8 @@
 
 
 def kernel(
-    n, ng, given, out, mine, before, own, from_left, from_right, to_right, to_left,
-    kept, to_before, from_next, m_sem, x_send, x_recv, s_send, s_recv,
+    n, ng, given, out, mine, before, following, own, from_left, from_right, to_right, to_left,
+    kept, to_before, from_next, m_sem, x_send, x_recv, y_send, y_recv, s_send, s_recv,
     r_send, r_recv, l_send, l_recv,
 ):
     z = lax.axis_index("group")
@@ -28,6 +28,7 @@
     blocks = triangle(rows)
     first = [i * (i + 1) // 2 for i in range(rows)]
     groups = [(i, 0, i + 1) for i in range(rows - 1)]
+    early = list(groups)
     groups += [(rows - 1, 0, rows - 2), (rows - 1, rows - 2, 2)]
 
     has_left, has_right = z > 0, z < n - 1
@@ -67,6 +68,17 @@
             device_id_type=MESH,
         )
 
+    def follower_copy(i):
+        span = pl.ds(i * B, B)
+        return pltpu.make_async_remote_copy(
+            src_ref=mine.at[span],
+            dst_ref=following.at[span],
+            send_sem=y_send.at[i],
+            recv_sem=y_recv.at[i],
+            device_id={"genome": g - 1},
+            device_id_type=MESH,
+        )
+
     def score_copy():
         return pltpu.make_async_remote_copy(
             src_ref=to_before,
@@ -97,17 +109,18 @@
             device_id_type=MESH,
         )
 
-    def products(i):
+    def products(ref, i, add):
         band = lax.dot_general(
-            mine[pl.ds(i * B, B), :],
-            mine[pl.ds(0, (i + 1) * B), :],
+            ref[pl.ds(i * B, B), :],
+            ref[pl.ds(0, (i + 1) * B), :],
             (((1,), (1,)), ((), ())),
             preferred_element_type=jnp.float32,
         )
         for j in range(i + 1):
-            own[first[i] + j] = band[:, j * B : (j + 1) * B]
-
-    def scored(group):
+            block = band[:, j * B : (j + 1) * B]
+            own[first[i] + j] = own[first[i] + j] + block if add else block
+
+    def scored(group, returned, here):
         i, j, count = group
         parts = []
         for k in range(j, j + count):
@@ -130,25 +143,43 @@
             )
             total[...] += jnp.sum(weighed, axis=0, keepdims=True)
 
-        @pl.when(has_before)
-        def _():
-            if group == groups[0]:
-                for k in range(rows):
-                    row_copy(k).wait_recv()
-            add(to_before, before)
-
-        add(kept, mine)
+        if returned and group in early:
+
+            @pl.when(has_before)
+            def _():
+                if group == early[0]:
+                    for k in range(rows):
+                        row_copy(k).wait_recv()
+                add(to_before, before)
+                if group == early[-1]:
+                    score_copy().start()
+
+        if here:
+            add(kept, mine)
 
     for i in range(rows):
         load(i).wait()
 
-    products(0)
+    @pl.when(has_before)
+    def _():
+        for i in range(rows):
+            follower_copy(i).start()
+
+    products(mine, 0, False)
     kept[...] = jnp.zeros_like(kept)
     to_before[...] = jnp.zeros_like(to_before)
     pending = list(groups)
     at_end = (z == 0) | (z == n - 1)
 
     for t in range(len(blocks) + SKEW * (n - 1)):
+        if t == first[rows - 1]:
+
+            @pl.when(has_next)
+            def _():
+                for i in range(rows):
+                    follower_copy(i).wait_recv()
+                products(following, rows - 1, True)
+
         c = t - SKEW * z
 
         @pl.when(has_right & (c >= 0) & (c < len(blocks)))
@@ -182,9 +213,9 @@
             left_copy(d).start()
 
         if t in first[: rows - 1]:
-            products(first.index(t) + 1)
-
-        if t == 1:
+            products(mine, first.index(t) + 1, False)
+
+        if t == 4:
 
             @pl.when(has_next)
             def _():
@@ -217,18 +248,16 @@
 
             @pl.when(at_end)
             def _():
-                scored(group)
+                scored(group, True, True)
 
             pending.pop(0)
 
     @pl.when(jnp.logical_not(at_end))
     def _():
+        for group in early:
+            scored(group, True, False)
         for group in groups:
-            scored(group)
-
-    @pl.when(has_before)
-    def _():
-        score_copy().start()
+            scored(group, False, True)
 
     @pl.when(has_next)
     def _():
@@ -245,6 +274,8 @@
     @pl.when(has_before)
     def _():
         score_copy().wait_send()
+        for i in range(rows):
+            follower_copy(i).wait_send()
 
     @pl.when(has_right)
     def _():
@@ -274,6 +305,7 @@
             scratch_shapes=[
                 pltpu.VMEM((samples, width), jnp.bfloat16),
                 pltpu.VMEM((samples, width), jnp.bfloat16),
+                pltpu.VMEM((samples, width), jnp.bfloat16),
                 pltpu.VMEM((steps, B, B), jnp.float32),
                 sent,
                 sent,
@@ -282,6 +314,8 @@
                 line,
                 line,
                 line,
+                pltpu.SemaphoreType.DMA((rows,)),
+                pltpu.SemaphoreType.DMA((rows,)),
                 pltpu.SemaphoreType.DMA((rows,)),
                 pltpu.SemaphoreType.DMA((rows,)),
                 pltpu.SemaphoreType.DMA((rows,)),

time: 27.8 us -> 25.5 us (0.917)
  the two profiles are of different devices: /device:TPU:1 before, /device:TPU:0 now
where the time goes in v7:
time: 25.5 us; the launch traced here: 25.4 us
  Pallas kernels  24.8 us (97%)
  other arithmetic  0.6 us (2%)
    pallas_call x1, Pallas kernels, per_device(): pl.pallas_call(functools.partial(kernel, n, ng), out_shape=jax.ShapeDtype...  24.8 us
    pallas_call x1, other arithmetic, per_device(): pl.pallas_call(functools.partial(kernel, n, ng), out_shape=jax.ShapeDtype...  0.6 us

profile of v7, /device:TPU:0, one launch (start us, length us, event | category | flops | bytes accessed | tf_op | source)
XLA Modules:
  0.0 25.4 jit_solution(13194341748595509568)
XLA Ops:
  0.0 24.8 %shard_map.17 = f32[1,384]{1,0:T(1,128)S(1)} custom-call(bf16[640,384]{1,0:T(8,128)(2,1)} %given.1), custom_call_target="tpu_custom_call" | custom-call | tf_op jit(solution)/shard_map/pallas_call | solution.py:300
  24.8 0.6 %reduce = f32[384]{0:T(512)} reduce(f32[1,384]{1,0:T(1,128)S(1)} %shard_map.17, f32[]{:T(128)} %constant), dimensions={0}, to_apply=%pallas_call.3.reduce_sub_computation | reduce | bytes 3076 | tf_op jit(solution)/shard_map/pallas_call | solution.py:300

commit v8 on v7

--- a/solution.py
+++ b/solution.py
@@ -27,9 +27,11 @@
     rows = samples // B
     blocks = triangle(rows)
     first = [i * (i + 1) // 2 for i in range(rows)]
-    groups = [(i, 0, i + 1) for i in range(rows - 1)]
+    groups = [(i, 0, i + 1) for i in range(rows - 1)] + [(rows - 1, 0, rows - 3)]
     early = list(groups)
-    groups += [(rows - 1, 0, rows - 2), (rows - 1, rows - 2, 2)]
+    late = (rows - 1, rows - 3, 3)
+    groups.append(late)
+    late_step = first[rows - 1] + late[1]
 
     has_left, has_right = z > 0, z < n - 1
     has_before, has_next = g > 0, g < ng - 1
@@ -52,6 +54,23 @@
 
     for i in range(rows):
         load(i).start()
+
+    def products(ref, group, add):
+        i, low, count = group
+        band = lax.dot_general(
+            ref[pl.ds(i * B, B), :],
+            ref[pl.ds(low * B, count * B), :],
+            (((1,), (1,)), ((), ())),
+            preferred_element_type=jnp.float32,
+        )
+        for k in range(count):
+            b = first[i] + low + k
+            block = band[:, k * B : (k + 1) * B]
+            own[b] = own[b] + block if add else block
+
+    for i in range(2):
+        load(i).wait()
+        products(mine, (i, 0, i + 1), False)
 
     peers = jnp.minimum(z, 1) + jnp.minimum(n - 1 - z, 1)
     peers = peers + jnp.minimum(g, 1) + jnp.minimum(ng - 1 - g, 1)
@@ -108,17 +127,6 @@
             device_id={"group": z - 1},
             device_id_type=MESH,
         )
-
-    def products(ref, i, add):
-        band = lax.dot_general(
-            ref[pl.ds(i * B, B), :],
-            ref[pl.ds(0, (i + 1) * B), :],
-            (((1,), (1,)), ((), ())),
-            preferred_element_type=jnp.float32,
-        )
-        for j in range(i + 1):
-            block = band[:, j * B : (j + 1) * B]
-            own[first[i] + j] = own[first[i] + j] + block if add else block
 
     def scored(group, returned, here):
         i, j, count = group
@@ -157,28 +165,28 @@
         if here:
             add(kept, mine)
 
-    for i in range(rows):
+    for i in range(2, rows):
         load(i).wait()
 
     @pl.when(has_before)
     def _():
-        for i in range(rows):
+        for i in range(late[1], rows):
             follower_copy(i).start()
 
-    products(mine, 0, False)
     kept[...] = jnp.zeros_like(kept)
     to_before[...] = jnp.zeros_like(to_before)
     pending = list(groups)
     at_end = (z == 0) | (z == n - 1)
 
     for t in range(len(blocks) + SKEW * (n - 1)):
-        if t == first[rows - 1]:
-
-            @pl.when(has_next)
-            def _():
-                for i in range(rows):
+        inner = (t - late_step) // SKEW
+        if t >= late_step and (t - late_step) % SKEW == 0 and inner <= (n - 1) // 2:
+
+            @pl.when(has_next & (jnp.minimum(z, n - 1 - z) == inner))
+            def _():
+                for i in range(late[1], rows):
                     follower_copy(i).wait_recv()
-                products(following, rows - 1, True)
+                products(following, late, True)
 
         c = t - SKEW * z
 
@@ -212,10 +220,11 @@
 
             left_copy(d).start()
 
-        if t in first[: rows - 1]:
-            products(mine, first.index(t) + 1, False)
-
-        if t == 4:
+        if t in first[1 : rows - 1]:
+            i = first.index(t) + 1
+            products(mine, (i, 0, i + 1), False)
+
+        if t == 2:
 
             @pl.when(has_next)
             def _():
@@ -250,12 +259,19 @@
             def _():
                 scored(group, True, True)
 
+            if group[0] < rows - 2:
+
+                @pl.when(jnp.logical_not(at_end))
+                def _():
+                    scored(group, True, False)
+
             pending.pop(0)
 
     @pl.when(jnp.logical_not(at_end))
     def _():
         for group in early:
-            scored(group, True, False)
+            if group[0] >= rows - 2:
+                scored(group, True, False)
         for group in groups:
             scored(group, False, True)
 
@@ -274,7 +290,7 @@
     @pl.when(has_before)
     def _():
         score_copy().wait_send()
-        for i in range(rows):
+        for i in range(late[1], rows):
             follower_copy(i).wait_send()
 
     @pl.when(has_right)

time: 25.5 us -> 25.8 us (1.012)
  the two profiles are of different devices: /device:TPU:0 before, /device:TPU:1 now
where the time goes in v8:
time: 25.8 us; the launch traced here: 25.6 us
  Pallas kernels  25 us (97%)
  other arithmetic  0.6 us (2%)
    pallas_call x1, Pallas kernels, per_device(): pl.pallas_call(functools.partial(kernel, n, ng), out_shape=jax.ShapeDtype...  25 us
    pallas_call x1, other arithmetic, per_device(): pl.pallas_call(functools.partial(kernel, n, ng), out_shape=jax.ShapeDtype...  0.6 us

profile of v8, /device:TPU:1, one launch (start us, length us, event | category | flops | bytes accessed | tf_op | source)
XLA Modules:
  0.0 25.6 jit_solution(5451146649535581477)
XLA Ops:
  0.0 25.0 %shard_map.17 = f32[1,384]{1,0:T(1,128)S(1)} custom-call(bf16[640,384]{1,0:T(8,128)(2,1)} %given.1), custom_call_target="tpu_custom_call" | custom-call | tf_op jit(solution)/shard_map/pallas_call | solution.py:316
  25.0 0.6 %reduce = f32[384]{0:T(512)} reduce(f32[1,384]{1,0:T(1,128)S(1)} %shard_map.17, f32[]{:T(128)} %constant), dimensions={0}, to_apply=%pallas_call.3.reduce_sub_computation | reduce | bytes 3076 | tf_op jit(solution)/shard_map/pallas_call | solution.py:316

commit v9 on v8

--- a/solution.py
+++ b/solution.py
@@ -165,14 +165,6 @@
         if here:
             add(kept, mine)
 
-    for i in range(2, rows):
-        load(i).wait()
-
-    @pl.when(has_before)
-    def _():
-        for i in range(late[1], rows):
-            follower_copy(i).start()
-
     kept[...] = jnp.zeros_like(kept)
     to_before[...] = jnp.zeros_like(to_before)
     pending = list(groups)
@@ -188,6 +180,22 @@
                     follower_copy(i).wait_recv()
                 products(following, late, True)
 
+        d = t - SKEW * (n - 1 - z)
+
+        @pl.when(has_left & (d >= 0) & (d < len(blocks)))
+        def _():
+            @pl.when(has_right)
+            def _():
+                left_copy(d).wait_recv()
+                total = own[d] + from_right[d].astype(jnp.float32)
+                to_left[d] = total.astype(to_left.dtype)
+
+            @pl.when(z == n - 1)
+            def _():
+                to_left[d] = own[d].astype(to_left.dtype)
+
+            left_copy(d).start()
+
         c = t - SKEW * z
 
         @pl.when(has_right & (c >= 0) & (c < len(blocks)))
@@ -204,21 +212,14 @@
 
             right_copy(c).start()
 
-        d = t - SKEW * (n - 1 - z)
-
-        @pl.when(has_left & (d >= 0) & (d < len(blocks)))
-        def _():
-            @pl.when(has_right)
-            def _():
-                left_copy(d).wait_recv()
-                total = own[d] + from_right[d].astype(jnp.float32)
-                to_left[d] = total.astype(to_left.dtype)
-
-            @pl.when(z == n - 1)
-            def _():
-                to_left[d] = own[d].astype(to_left.dtype)
-
-            left_copy(d).start()
+        if t == 0:
+            for i in range(2, rows):
+                load(i).wait()
+
+            @pl.when(has_before)
+            def _():
+                for i in range(late[1], rows):
+                    follower_copy(i).start()
 
         if t in first[1 : rows - 1]:
             i = first.index(t) + 1

time: 25.8 us -> 25.9 us (level)
  no operation moved by 1% of the time
where the time goes in v9:
time: 25.9 us; the launch traced here: 25.7 us
  Pallas kernels  25.1 us (97%)
  other arithmetic  0.6 us (2%)
    pallas_call x1, Pallas kernels, per_device(): pl.pallas_call(functools.partial(kernel, n, ng), out_shape=jax.ShapeDtype...  25.1 us
    pallas_call x1, other arithmetic, per_device(): pl.pallas_call(functools.partial(kernel, n, ng), out_shape=jax.ShapeDtype...  0.6 us

profile of v9, /device:TPU:1, one launch (start us, length us, event | category | flops | bytes accessed | tf_op | source)
XLA Modules:
  0.0 25.7 jit_solution(2239220773789107957)
XLA Ops:
  0.0 25.1 %shard_map.17 = f32[1,384]{1,0:T(1,128)S(1)} custom-call(bf16[640,384]{1,0:T(8,128)(2,1)} %given.1), custom_call_target="tpu_custom_call" | custom-call | tf_op jit(solution)/shard_map/pallas_call | solution.py:317
  25.1 0.6 %reduce = f32[384]{0:T(512)} reduce(f32[1,384]{1,0:T(1,128)S(1)} %shard_map.17, f32[]{:T(128)} %constant), dimensions={0}, to_apply=%pallas_call.3.reduce_sub_computation | reduce | bytes 3076 | tf_op jit(solution)/shard_map/pallas_call | solution.py:317

commit v10 on v9

--- a/solution.py
+++ b/solution.py
@@ -27,10 +27,10 @@
     rows = samples // B
     blocks = triangle(rows)
     first = [i * (i + 1) // 2 for i in range(rows)]
-    groups = [(i, 0, i + 1) for i in range(rows - 1)] + [(rows - 1, 0, rows - 3)]
+    groups = [(i, 0, i + 1) for i in range(rows - 1)]
     early = list(groups)
-    late = (rows - 1, rows - 3, 3)
-    groups.append(late)
+    late = (rows - 1, 0, rows)
+    groups += [(rows - 1, 0, rows - 2), (rows - 1, rows - 2, 2)]
     late_step = first[rows - 1] + late[1]
 
     has_left, has_right = z > 0, z < n - 1

time: 25.9 us -> 25.4 us (0.981)
  the two profiles are of different devices: /device:TPU:1 before, /device:TPU:0 now
where the time goes in v10:
time: 25.4 us; the launch traced here: 25.2 us
  Pallas kernels  24.6 us (97%)
  other arithmetic  0.6 us (2%)
    pallas_call x1, Pallas kernels, per_device(): pl.pallas_call(functools.partial(kernel, n, ng), out_shape=jax.ShapeDtype...  24.6 us
    pallas_call x1, other arithmetic, per_device(): pl.pallas_call(functools.partial(kernel, n, ng), out_shape=jax.ShapeDtype...  0.6 us

profile of v10, /device:TPU:0, one launch (start us, length us, event | category | flops | bytes accessed | tf_op | source)
XLA Modules:
  0.0 25.2 jit_solution(11536204465885098216)
XLA Ops:
  0.0 24.6 %shard_map.17 = f32[1,384]{1,0:T(1,128)S(1)} custom-call(bf16[640,384]{1,0:T(8,128)(2,1)} %given.1), custom_call_target="tpu_custom_call" | custom-call | tf_op jit(solution)/shard_map/pallas_call | solution.py:317
  24.6 0.6 %reduce = f32[384]{0:T(512)} reduce(f32[1,384]{1,0:T(1,128)S(1)} %shard_map.17, f32[]{:T(128)} %constant), dimensions={0}, to_apply=%pallas_call.3.reduce_sub_computation | reduce | bytes 3076 | tf_op jit(solution)/shard_map/pallas_call | solution.py:317

commit v11 on v10

--- a/solution.py
+++ b/solution.py
@@ -225,7 +225,7 @@
             i = first.index(t) + 1
             products(mine, (i, 0, i + 1), False)
 
-        if t == 2:
+        if t == 6:
 
             @pl.when(has_next)
             def _():

time: 25.4 us -> 25.8 us (1.016)
  the two profiles are of different devices: /device:TPU:0 before, /device:TPU:1 now
where the time goes in v11:
time: 25.8 us; the launch traced here: 25.7 us
  Pallas kernels  25.1 us (97%)
  other arithmetic  0.6 us (2%)
    pallas_call x1, Pallas kernels, per_device(): pl.pallas_call(functools.partial(kernel, n, ng), out_shape=jax.ShapeDtype...  25.1 us
    pallas_call x1, other arithmetic, per_device(): pl.pallas_call(functools.partial(kernel, n, ng), out_shape=jax.ShapeDtype...  0.6 us

profile of v11, /device:TPU:1, one launch (start us, length us, event | category | flops | bytes accessed | tf_op | source)
XLA Modules:
  0.0 25.7 jit_solution(2568464968707854678)
XLA Ops:
  0.0 25.1 %shard_map.17 = f32[1,384]{1,0:T(1,128)S(1)} custom-call(bf16[640,384]{1,0:T(8,128)(2,1)} %given.1), custom_call_target="tpu_custom_call" | custom-call | tf_op jit(solution)/shard_map/pallas_call | solution.py:317
  25.1 0.6 %reduce = f32[384]{0:T(512)} reduce(f32[1,384]{1,0:T(1,128)S(1)} %shard_map.17, f32[]{:T(128)} %constant), dimensions={0}, to_apply=%pallas_call.3.reduce_sub_computation | reduce | bytes 3076 | tf_op jit(solution)/shard_map/pallas_call | solution.py:317
